TPU v7x, 512 devices: a whole 4x4x16 slice. The times are simulated.
512 devices in a mesh: cube: 512 (over x, y, z, core).
Axes of the slice: x: 4, y: 4, z: 16, core: 2. Of those that a mesh axis runs over, the one named last changes fastest.
Arguments:
- points: float32 [8192, 3, 512], P('cube'), may hold values from -1 to 1
- charges: float32 [8192, 4, 512], P('cube'), may hold values from -0.15 to 0.15
- leaf_density: float32 [8192, 4, 296], P('cube'), may hold values from -6 to 6
- leaf_octant: int32 [8192], P('cube'), may hold values from 0 to 511, as said below
- user_lists: int32 [512, 2, 4], P('cube'), may hold values from 0 to 15
- near_leaves: int32 [8192, 4], P('cube'), may hold values from 0 to 23
- near_codes: int32 [8192, 4], P('cube'), may hold values from 0 to 25
- upward_map: float32 [296, 296], replicated, may hold values from -0.09375 to 0.09375
- lower_map: float32 [296, 296], replicated, may hold values from -0.25 to 0.25
- upper_map: float32 [296, 296], replicated, may hold values from -0.25 to 0.25
- downward_map: float32 [296, 296], replicated, may hold values from -0.375 to 0.375
Outputs:
- potential: float32 [8192, 4, 512], P('cube')
Inputs may be any that keep to these rules, and one draw needn't show every extreme that they name: user_lists[d, 0] names leaf boxes of partition d - 1 and user_lists[d, 1] of partition d + 1, as indices within that partition; entries of missing partitions are unused. `near_leaves`: rows of the near set: own boxes first, then the 4 read from below, then the 4 read from above. `near_codes`: one of the 26 neighbour directions. `leaf_octant`: any shared octant; some leaf boxes of every partition lie in arbitrary octants, which may be held anywhere along the axis.
All inputs are finite; a program needn't handle non-finite values.
Results may differ from a plain program's by a relative error of at most 0.0003.
Values sent between devices are 32-bit elements; how exact they have to be, the bound alone decides.
A program may use at most 64 MiB of HBM per device.

v0:
```python
import math

import jax
import jax.numpy as jnp
import numpy as np
from jax import lax
from jax.sharding import PartitionSpec as P

EQ_ORDER = 8


inv_four_pi = 1.0 / (4.0 * math.pi)
soften = 0.01


def passed_along(value, axis, steps):
    count = lax.axis_size(axis)
    initial, last = (max(0, -steps), min(count, count - steps))
    return lax.ppermute(value, axis, [(source, source + steps) for source in range(initial, last)])


def surface_table():
    spacing = np.linspace(-1.0, 1.0, EQ_ORDER)
    mesh_x, mesh_y, mesh_z = np.meshgrid(spacing, spacing, spacing, indexing="ij")
    lattice = np.stack([mesh_x.ravel(), mesh_y.ravel(), mesh_z.ravel()], 0)
    on_boundary = np.max(np.abs(lattice), axis=0) > 0.999
    return lattice[:, on_boundary] * 2.95


def kernel(targets, sources):
    separation = targets[..., :, :, None] - sources[..., :, None, :]
    return inv_four_pi / jnp.sqrt(jnp.sum(separation * separation, axis=-3) + soften)


def direction_offsets(codes):
    shifted = codes + (codes >= 13).astype(jnp.int32)
    parts_xyz = jnp.stack([shifted // 9 - 1, shifted // 3 % 3 - 1, shifted % 3 - 1], -1)
    return 2.0 * parts_xyz.astype(jnp.float32)


def translate(octant_lower, octant_upper, lower_map, upper_map):
    highest = lax.Precision.HIGHEST
    return jnp.einsum("oqs,st->oqt", octant_lower, lower_map, precision=highest) + jnp.einsum(
        "oqs,st->oqt", octant_upper, upper_map, precision=highest
    )


def body(
    points,
    charges,
    leaf_density,
    leaf_octant,
    user_lists,
    near_leaves,
    near_codes,
    upward_map,
    lower_map,
    upper_map,
    downward_map,
):
    highest = lax.Precision.HIGHEST
    shared = lax.axis_size("cube")
    leaf_count = points.shape[0]
    leaf_part = jnp.einsum("lqs,st->lqt", leaf_density, upward_map, precision=highest)
    member = (leaf_octant[None, :] == jnp.arange(shared, dtype=jnp.int32)[:, None]).astype(
        jnp.float32
    )
    partial_value = jnp.einsum("ol,lqs->oqs", member, leaf_part, precision=highest)
    owned_sum = lax.psum_scatter(partial_value, "cube", scatter_dimension=0, tiled=True)
    octant_lower = passed_along(owned_sum, "cube", 1)
    octant_upper = passed_along(owned_sum, "cube", -1)
    owned_local = translate(octant_lower, octant_upper, lower_map, upper_map)
    shard_rows = lax.all_gather(owned_local, "cube", axis=0, tiled=True)
    octant_ids = jnp.arange(shard_rows.shape[0], dtype=jnp.int32)
    chosen = (leaf_octant[:, None] == octant_ids[None, :]).astype(jnp.float32)
    selected = jnp.einsum("lo,oqs->lqs", chosen, shard_rows, precision=highest)
    leaf_local = jnp.einsum("lqs,st->lqt", selected, downward_map, precision=highest)
    wanted = user_lists[0]
    below_points, below_charges = passed_along((points, charges), "cube", 1)
    above_points, above_charges = passed_along((points, charges), "cube", -1)
    lower_points = below_points[wanted[0]]
    lower_charges = below_charges[wanted[0]]
    upper_points = above_points[wanted[1]]
    upper_charges = above_charges[wanted[1]]
    set_points = jnp.concatenate([points, lower_points, upper_points], 0)
    set_charges = jnp.concatenate([charges, lower_charges, upper_charges], 0)
    surface = jnp.asarray(surface_table(), jnp.float32)

    def block(inputs):
        targets, charge_block, local_block, neighbours, codes = inputs
        totals_near = jnp.einsum(
            "lps,lqs->lqp", kernel(targets, targets), charge_block, precision=highest
        )
        offsets = direction_offsets(codes)
        for slot_index in range(neighbours.shape[1]):
            rows = neighbours[:, slot_index]
            sources = set_points[rows] + offsets[:, slot_index, :, None]
            totals_near = totals_near + jnp.einsum(
                "lps,lqs->lqp", kernel(targets, sources), set_charges[rows], precision=highest
            )
        far_field = jnp.einsum(
            "lps,lqs->lqp", kernel(targets, surface), local_block, precision=highest
        )
        return far_field + totals_near

    block_width = math.gcd(leaf_count, 2)
    groups = leaf_count // block_width
    stacked = tuple(
        (
            array_item.reshape((groups, block_width) + array_item.shape[1:])
            for array_item in (points, charges, leaf_local, near_leaves, near_codes)
        )
    )
    result = lax.map(block, stacked)
    return result.reshape(charges.shape)


def solution(mesh):
    in_specs = (
        P("cube", None, None),
        P("cube", None, None),
        P("cube", None, None),
        P("cube"),
        P("cube", None, None),
        P("cube", None),
        P("cube", None),
        P(),
        P(),
        P(),
        P(),
    )
    out_specs = P("cube", None, None)
    return jax.shard_map(body, mesh=mesh, in_specs=in_specs, out_specs=out_specs, check_vma=False)
```

profile of v0, /device:TPU:1, one launch (start us, length us, event | category | flops | bytes accessed | tf_op | source)
XLA Modules:
  0.0 965.7 jit_solution(9954740913374649261)
XLA Ops:
  11.1 3.7 copy.52
  14.9 489.0 %all-reduce.3.cloned.1.call-done = f32[512,4,296]{2,1,0:T(4,128)} async-done(((f32[512,4,296]{2,1,0:T(4,128)}), f32[512,4,296]{2,1,0:T(4,128)}) %all-reduce.3.cloned.1.call-update) | async-done | bytes 2424848
  504.6 4.0 collective-permute-start.1
  512.8 3.8 collective-permute-start.4
  518.5 3.6 collective-permute-start.2
  529.1 180.7 %all-gather.4.cloned.1.call-done = f32[512,4,296]{2,1,0:T(4,128)} async-done(((f32[1,4,296]{2,1,0:T(4,128)}), f32[512,4,296]{2,1,0:T(4,128)}) %all-gather.4.cloned.1.call-update) | async-done | bytes 2424848 | tf_op jit(solution)/shard_map/all_gather | solution.py:73
  713.4 244.8 %while.14 = (s32[]{:T(128)}, f32[8,2,4,512]{3,2,1,0:T(4,128)S(1)}, f32[8,2,4,296]{3,2,1,0:T(4,128)S(1)}, f32[8,2,3,512]{3,2,1,0:T(4,128)S(1)}, f32[8,2,4,512]{3,...) while((s32[]{:T(128)}, f32[8,2,4,512]{3,2,1,0:T(4,128)S(1)}, ...), condition=%wide.region_8.9_spmd.clone, body=%wide.region_1.8_spmd.sunk.clone.sunk | while | flops 169660768 | bytes 24118876 | solution.py:114
  716.9 7.9 multiply_reduce_fusion.6
  725.4 3.5 fusion.159
  737.5 3.5 fusion.157
  747.5 7.9 multiply_reduce_fusion.6
  764.1 3.5 fusion.158
  778.1 7.9 multiply_reduce_fusion.6
  790.6 3.5 fusion.160
  808.6 7.9 multiply_reduce_fusion.6
  825.2 3.5 fusion.158
  829.3 3.5 fusion.157
  839.2 7.9 multiply_reduce_fusion.6
  851.7 3.5 fusion.160
  855.8 3.5 fusion.158
  869.8 7.9 multiply_reduce_fusion.6
  878.3 3.5 fusion.159
  900.4 7.9 multiply_reduce_fusion.6
  931.0 7.9 multiply_reduce_fusion.6
  (296 shorter events, 172.3 us)
Async XLA Ops:
  6.5 1.0 copy-start
  6.5 497.4 %all-reduce.3.cloned.1.call-start = ((), (), s32[]{:S(2)}) async-start(), calls=%async_computation.1 | async-start | bytes 6291456
  14.8 495.8 %copy-start.1 = (f32[296,296]{1,0:T(8,128)S(1)}, f32[296,296]{1,0:T(8,128)}, u32[]{:S(2)}) copy-start(f32[296,296]{1,0:T(8,128)} %param.23) | copy-start | bytes 1051396
  14.8 496.9 %copy-start.3 = (f32[296,296]{1,0:T(8,128)S(1)}, f32[296,296]{1,0:T(8,128)}, u32[]{:S(2)}) copy-start(f32[296,296]{1,0:T(8,128)} %param.22) | copy-start | bytes 1051396
  14.8 497.9 %copy-start.6 = (f32[16,3,512]{2,0,1:T(8,128)S(1)}, f32[16,3,512]{2,0,1:T(8,128)}, u32[]{:S(2)}) copy-start(f32[16,3,512]{2,0,1:T(8,128)} %param.14) | copy-start | bytes 294916
  14.8 503.7 %copy-start.4 = (f32[16,4,512]{2,1,0:T(4,128)S(1)}, f32[16,4,512]{2,1,0:T(4,128)}, u32[]{:S(2)}) copy-start(f32[16,4,512]{2,1,0:T(4,128)} %param.15) | copy-start | bytes 393220
  14.8 509.3 %copy-start.10 = (s32[1,2,4]{2,1,0:T(2,128)S(1)}, s32[1,2,4]{2,1,0:T(2,128)}, u32[]{:S(2)}) copy-start(s32[1,2,4]{2,1,0:T(2,128)} %param.18) | copy-start | bytes 100
  14.8 509.3 %copy-start.7 = (s32[16,4]{0,1:T(4,128)S(1)}, s32[16,4]{0,1:T(4,128)}, u32[]{:S(2)}) copy-start(s32[16,4]{0,1:T(4,128)} %param.19) | copy-start | bytes 772
  14.8 509.4 %copy-start.8 = (s32[16,4]{0,1:T(4,128)S(1)}, s32[16,4]{0,1:T(4,128)}, u32[]{:S(2)}) copy-start(s32[16,4]{0,1:T(4,128)} %param.20) | copy-start | bytes 772
  14.8 695.0 %copy-start.9 = (s32[16]{0:T(128)S(1)}, s32[16]{0:T(128)}, u32[]{:S(2)}) copy-start(s32[16]{0:T(128)} %param.17) | copy-start | bytes 196
  14.9 695.0 %all-gather.4.cloned.1.call-start = ((), (), s32[]{:S(2)}) async-start(), calls=%async_computation | async-start | bytes 3151872 | tf_op jit(solution)/shard_map/all_gather | solution.py:73
  504.6 6.0 collective-permute-start.1
  508.6 3.1 collective-permute-start
  512.8 11.6 %collective-permute-start.4 = (f32[16,3,512]{2,1,0:T(4,128)S(1)}, f32[16,3,512]{2,1,0:T(4,128)S(1)}, u32[]{:S(2)}, u32[]{:S(2)}) collective-permute-start(f32[16,3,512]{2,1,0:T(4,128)S(1)} %copy.54), channel_id=1, source_target_pairs={{0,1},{1,2},{2,3},{3,4},{4,5},{5,6},{6,7},{7,8},{8,9},{9,10},{10,1... | collective-permute-start | bytes 294920 | tf_op jit(solution)/shard_map/ppermute | solution.py:19
  516.6 8.3 collective-permute-start.5
  518.5 7.0 collective-permute-start.2
  522.2 6.3 collective-permute-start.3
  525.5 187.4 %copy-start.2 = (f32[296,296]{1,0:T(8,128)S(1)}, f32[296,296]{1,0:T(8,128)}, u32[]{:S(2)}) copy-start(f32[296,296]{1,0:T(8,128)} %param.24) | copy-start | bytes 1051396
  529.1 184.3 %copy-start.5 = (f32[3,296]{1,0:T(4,128)S(1)}, f32[3,296]{1,0:T(4,128)}, u32[]{:S(2)}) copy-start(f32[3,296]{1,0:T(4,128)} %constant.270) | copy-start | bytes 10660
  958.2 0.7 copy-start.11
Sparse Core Ops, SparseCore 0:
  15.0 488.8 all-reduce.2
  512.8 197.0 all-gather.3
where the time goes:
time: 967 us; the launch traced here: 966 us
  waiting for transfers between devices  673 us (70%)
  matrix products  141 us (15%)
  other arithmetic  71.1 us (7%)
  local copies, waits for them, and re-layouts  49.4 us (5%)
  starting transfers between devices  17.3 us (2%)
  between operations  13.7 us (1%)
    unnamed x3, waiting for transfers between devices  489 us
    all_gather x1, waiting for transfers between devices, body(): shard_rows = lax.all_gather(owned_local, 'cube', axis=0, tiled=True)  181 us
    dot_general x32, matrix products, block(): jnp.einsum('lps,lqs->lqp', kernel(targets, sources), set_charges[rows], p...  111 us
    reduce_sum x16, other arithmetic, kernel(): jnp.sum(separation * separation, axis=-3) + soften  66.4 us
  transfers between devices with their start and end apart: 8, of which 4 were waited for; matrix products, arithmetic and copies ran while one was open for 0% of the time, Pallas kernels for 0%

commit v1 on v0

v1 whole, which is shorter than its diff:
```python
import functools
import math

import jax
import jax.numpy as jnp
import numpy as np
from jax import lax
from jax.experimental import pallas as pl
from jax.experimental.pallas import tpu as pltpu
from jax.sharding import PartitionSpec as P

EQ_ORDER = 8
INV_FOUR_PI = 1.0 / (4.0 * math.pi)
SOFTEN = 0.01
LB = 16
UH = 4
K = 4
Q = 4
S = 296
SP = 384
PTS = 512
FAR = 304
ROWS = LB * Q
MESH = pl.DeviceIdType.MESH
F32 = jnp.float32
BF16 = jnp.bfloat16
NX, NY, NZ = 4, 4, 16
NG = 4


def surface_table():
    spacing = np.linspace(-1.0, 1.0, EQ_ORDER)
    mesh_x, mesh_y, mesh_z = np.meshgrid(spacing, spacing, spacing, indexing="ij")
    lattice = np.stack([mesh_x.ravel(), mesh_y.ravel(), mesh_z.ravel()], 0)
    on_boundary = np.max(np.abs(lattice), axis=0) > 0.999
    return lattice[:, on_boundary] * 2.95


def split3(v):
    a = v.astype(BF16).astype(F32)
    r = v - a
    b = r.astype(BF16).astype(F32)
    return a, b, r - b


def source_features(p, row):
    nsq = jnp.sum(p * p, axis=0, keepdims=True)
    u = jnp.where(row == 3, nsq, jnp.where(row == 4, 1.0, p))
    a, b, c = split3(u)
    return jnp.concatenate([a, a, b, b, a, c], axis=0)


def target_features(t, row):
    nsq = jnp.sum(t * t, axis=0, keepdims=True) + SOFTEN
    v = jnp.where(row == 3, 1.0, jnp.where(row == 4, nsq, -2.0 * t))
    a, b, c = split3(v)
    return jnp.concatenate([a, b, a, b, c, a], axis=0).astype(BF16)


def surface_features():
    pts = np.zeros((8, FAR), np.float32)
    pts[:3, :S] = surface_table().astype(np.float32)
    pts[:3, S:] = pts[:3, :1]
    u = pts.copy()
    u[3] = np.sum(pts * pts, axis=0)
    u[4] = 1.0
    a = u.astype(jnp.bfloat16).astype(np.float32)
    b = (u - a).astype(jnp.bfloat16).astype(np.float32)
    c = u - a - b
    return np.concatenate([a, a, b, b, a, c], axis=0).T.astype(jnp.bfloat16)


def pair_sum(feat, ft, weights):
    r2 = jnp.dot(feat, ft, preferred_element_type=F32)
    g = lax.rsqrt(r2)
    hi = g.astype(BF16)
    lo = (g - hi.astype(F32)).astype(BF16)
    return jnp.dot(weights, hi, preferred_element_type=F32) + jnp.dot(
        weights, lo, preferred_element_type=F32
    )


OCT, USER, NEAR, CODE = 0, LB, LB + 2 * UH, LB + 2 * UH + LB * K
N_META = CODE + LB * K


def kernel(
    meta, pts, ch, dens, up, low, upp, down, fsurf,
    out,
    xp, fs, cw, hp, hc, near, rbuf, p1, qb, p2, zb, table, sel, cfar,
    halo_s, halo_r, core_s, core_r, a_s, a_r, b_s, b_r, z_s, z_r,
    gz_s, gz_r, gb_s, gb_r, ga_s, ga_r, gc_s, gc_r,
):
    me = lax.axis_index("cube")
    count = 2 * NX * NY * NZ
    core = me % 2
    z = (me // 2) % NZ
    y = (me // (2 * NZ)) % NY
    x = me // (2 * NZ * NY)
    stride_x, stride_y = 2 * NZ * NY, 2 * NZ
    stride_a = stride_x * (1 - core) + stride_y * core
    stride_b = stride_y * (1 - core) + stride_x * core
    a = x * (1 - core) + y * core
    b = y * (1 - core) + x * core
    a_partner = y * (1 - core) + x * core
    partner = me + 1 - 2 * core
    oct_a = core * (NG * NG * NZ) + a * (NG * NZ)
    oct_b = oct_a + b * NZ
    oct_z = oct_b + z

    def peer_a(i):
        return me + ((a + i) % NG - a) * stride_a

    def peer_b(i):
        return me + ((b + i) % NG - b) * stride_b

    def peer_z(i):
        return me + ((z + i) % NZ - z) * 2

    def send(src, dst, s, r, dev):
        return pltpu.make_async_remote_copy(
            src_ref=src, dst_ref=dst, send_sem=s, recv_sem=r, device_id=(dev,), device_id_type=MESH
        )

    row8 = lax.broadcasted_iota(jnp.int32, (8, PTS), 0)

    barrier = pltpu.get_barrier_semaphore()

    def greet(dev):
        pl.semaphore_signal(barrier, inc=1, device_id=(dev,), device_id_type=MESH)

    greet(partner)
    for i in range(1, NG):
        greet(peer_a(i))
        greet(peer_b(i))

    def greet_z(i, _):
        greet(peer_z(i))
        return 0

    lax.fori_loop(1, NZ, greet_z, 0)
    n_greet = 1 + 2 * (NG - 1) + NZ - 1

    @pl.when(me > 0)
    def _():
        greet(me - 1)

    @pl.when(me < count - 1)
    def _():
        greet(me + 1)

    mine = a * 2 + core
    rbuf[mine] = jnp.zeros((ROWS + 8, SP), F32)
    for l in range(LB):
        rbuf[mine, Q * l : Q * l + Q, 0:S] = dens[l]
    lane = lax.broadcasted_iota(jnp.int32, (8, SP), 1) % ROWS
    keys = jnp.zeros((8, SP), jnp.int32)
    for l in range(LB):
        keys = jnp.where(lane // Q == l, meta[OCT + l], keys)
    rbuf[mine, ROWS : ROWS + 8, :] = (keys * Q + lane % Q).astype(F32)

    def prep(n, p, q):
        fs[n] = source_features(p, row8).T.astype(BF16)
        hi = q.astype(BF16).astype(F32)
        lo = q - hi
        cw[n] = jnp.concatenate([hi + pltpu.roll(lo, 4, 0), jnp.zeros((8, PTS), F32)], axis=0).astype(BF16)

    xp[...] = jnp.zeros(xp.shape, F32)

    def prep_own(n, _):
        xp[n, 0:3, :] = pts[n]
        xp[LB, 0:4, :] = ch[n] * INV_FOUR_PI
        prep(n, xp[n], xp[LB])
        return 0

    n_wait = n_greet + (me + count - 1) // count + (2 * count - 2 - me) // count
    pl.semaphore_wait(barrier, n_wait)

    def halo(i):
        dev = me + 1 - 2 * i
        return (
            send(pts, hp.at[i], halo_s.at[i], halo_r.at[i], dev),
            send(ch, hc.at[i], halo_s.at[2 + i], halo_r.at[2 + i], dev),
        )

    core_out = send(rbuf.at[mine], rbuf.at[a_partner * 2 + core], core_s, core_r, partner)
    core_in = send(rbuf.at[mine], rbuf.at[a * 2 + 1 - core], core_s, core_r, partner)
    core_out.start()

    @pl.when(me < count - 1)
    def _():
        for c in halo(0):
            c.start()

    @pl.when(me > 0)
    def _():
        for c in halo(1):
            c.start()

    lax.fori_loop(0, LB, prep_own, 0)

    def a_copy(i, at):
        return send(rbuf.at[pl.ds(at * 2, 2)], rbuf.at[pl.ds(at * 2, 2)], a_s.at[i], a_r.at[i], peer_a(i))

    def b_copy(i, chunk, at):
        return send(p1.at[pl.ds(chunk * NZ * Q, NZ * Q)], qb.at[at], b_s.at[i], b_r.at[i], peer_b(i))

    def z_copy(i, chunk, at):
        return send(p2.at[chunk], zb.at[at], z_s.at[i], z_r.at[i], peer_z(i))

    def gz_copy(i, o):
        return send(table.at[o], table.at[o], gz_s.at[i], gz_r.at[i], peer_z(i))

    def gb_copy(i, o):
        return send(table.at[pl.ds(o, NZ)], table.at[pl.ds(o, NZ)], gb_s.at[i], gb_r.at[i], peer_b(i))

    def ga_copy(i, o):
        return send(
            table.at[pl.ds(o, NG * NZ)], table.at[pl.ds(o, NG * NZ)], ga_s.at[i], ga_r.at[i], peer_a(i)
        )

    def gc_copy(c):
        half = NG * NG * NZ
        return send(table.at[pl.ds(c * half, half)], table.at[pl.ds(c * half, half)], gc_s, gc_r, partner)

    def step_a():
        core_in.wait_recv()
        for i in range(1, NG):
            a_copy(i, a).start()

    def step_b():
        for i in range(1, NG):
            a_copy(i, (a + NG - i) % NG).wait_recv()
        rows = lax.broadcasted_iota(jnp.int32, (NG * NZ * Q, 3 * ROWS), 0) + oct_a * Q
        rows = rows.astype(F32)
        p1[...] = jnp.zeros(p1.shape, F32)

        def add(j, _):
            member = jnp.where(rows == rbuf[j, ROWS : ROWS + 1, 0 : 3 * ROWS], 1.0, 0.0).astype(BF16)
            parts = jnp.concatenate(split3(rbuf[j, 0:ROWS, :]), axis=0).astype(BF16)
            p1[...] += jnp.dot(member, parts, preferred_element_type=F32)
            return 0

        lax.fori_loop(0, 2 * NG, add, 0)
        for i in range(1, NG):
            b_copy(i, (b + i) % NG, b).start()

    def step_z():
        total = p1[pl.ds(pl.multiple_of(b * NZ * Q, 8), NZ * Q), :]
        for i in range(1, NG):
            at = (b + NG - i) % NG
            b_copy(i, at, at).wait_recv()
            total = total + qb[at]
        for j in range(NZ):
            p2[j] = total[Q * j : Q * j + Q, :]

        def go(i, _):
            z_copy(i, (z + i) % NZ, z).start()
            return 0

        lax.fori_loop(1, NZ, go, 0)

    def step_gz():
        def take(i, total):
            at = (z + NZ - i) % NZ
            z_copy(i, at, at).wait_recv()
            return total + zb[at]

        table[oct_z] = lax.fori_loop(1, NZ, take, p2[z])

        def go(i, _):
            gz_copy(i, oct_z).start()
            return 0

        lax.fori_loop(1, NZ, go, 0)

    def step_gb():
        def take(i, _):
            gz_copy(i, oct_b + (z + NZ - i) % NZ).wait_recv()
            return 0

        lax.fori_loop(1, NZ, take, 0)
        for i in range(1, NG):
            gb_copy(i, oct_b).start()

    def step_ga():
        for i in range(1, NG):
            gb_copy(i, oct_a + (b + NG - i) % NG * NZ).wait_recv()
        for i in range(1, NG):
            ga_copy(i, oct_a).start()

    def step_gc():
        for i in range(1, NG):
            ga_copy(i, core * (NG * NG * NZ) + (a + NG - i) % NG * (NG * NZ)).wait_recv()
        gc_copy(core).start()

    def own_leaf(l, _):
        near[l] = pair_sum(fs[l], target_features(xp[l], row8), cw[l])

        @pl.when(l == OWN_AT[0])
        def _():
            step_a()

        @pl.when(l == OWN_AT[1])
        def _():
            step_b()

        return 0

    lax.fori_loop(0, LB, own_leaf, 0)

    for i in range(2):
        present = me > 0 if i == 0 else me < count - 1

        @pl.when(present)
        def _():
            for c in halo(i):
                c.wait_recv()

        @pl.when(jnp.logical_not(present))
        def _():
            hp[i] = jnp.zeros(hp.shape[1:], F32)
            hc[i] = jnp.zeros(hc.shape[1:], F32)

    for i in range(2):

        def prep_halo(j, _):
            n = meta[USER + i * UH + j]
            xp[LB + 1, 0:3, :] = hp[i, n]
            xp[LB, 0:4, :] = hc[i, n] * INV_FOUR_PI
            prep(LB + i * UH + j, xp[LB + 1], xp[LB])
            return 0

        lax.fori_loop(0, UH, prep_halo, 0)

    def near_leaf(l, _):
        acc = near[l]
        box = xp[l]
        for k in range(K):
            n = meta[NEAR + l * K + k]
            code = meta[CODE + l * K + k]
            code = jnp.where(code >= 13, code + 1, code)
            ox = (2 * (code // 9 - 1)).astype(F32)
            oy = (2 * ((code // 3) % 3 - 1)).astype(F32)
            oz = (2 * (code % 3 - 1)).astype(F32)
            off = jnp.where(row8 == 0, ox, jnp.where(row8 == 1, oy, jnp.where(row8 == 2, oz, 0.0)))
            acc = acc + pair_sum(fs[n], target_features(box - off, row8), cw[n])
        near[l] = acc
        for at, step in zip(NEAR_AT, (step_z, step_gz, step_gb, step_ga, step_gc)):

            @pl.when(l == at)
            def _():
                step()

        return 0

    lax.fori_loop(0, LB, near_leaf, 0)

    gc_copy(1 - core).wait_recv()
    n_oct = NX * NY * NZ * 2
    for l in range(LB):
        o = meta[OCT + l]
        below = jnp.where(o > 0, 1.0, 0.0).astype(F32)
        above = jnp.where(o < n_oct - 1, 1.0, 0.0).astype(F32)
        sel[Q * l : Q * l + Q, :] = table[jnp.maximum(o - 1, 0)] * below
        sel[ROWS + Q * l : ROWS + Q * l + Q, :] = table[jnp.minimum(o + 1, n_oct - 1)] * above
    highest = lax.Precision.HIGHEST
    t = jnp.dot(sel[:, 0:S], up[...], precision=highest, preferred_element_type=F32)
    w = jnp.dot(t[0:ROWS], low[...], precision=highest, preferred_element_type=F32) + jnp.dot(
        t[ROWS:], upp[...], precision=highest, preferred_element_type=F32
    )
    w = jnp.dot(w, down[...], precision=highest, preferred_element_type=F32) * INV_FOUR_PI
    hi = w.astype(BF16).astype(F32)
    lo = w - hi
    cfar[...] = jnp.zeros(cfar.shape, BF16)
    for t in range(LB // 2):
        pair = jnp.concatenate([hi[8 * t : 8 * t + 8], lo[8 * t : 8 * t + 8]], axis=0)
        cfar[t, :, 0:S] = pair.astype(BF16)

    def far_pair(t, _):
        for h in range(2):
            l = 2 * t + h
            far = pair_sum(fsurf[...], target_features(xp[l], row8), cfar[t, :, 0:FAR])
            far = far[0:8] + far[8:16]
            out[l] = far[4 * h : 4 * h + 4] + near[l, 0:4, :] + near[l, 4:8, :]
        return 0

    lax.fori_loop(0, LB // 2, far_pair, 0)

    core_out.wait_send()

    @pl.when(me < count - 1)
    def _():
        for c in halo(0):
            c.wait_send()

    @pl.when(me > 0)
    def _():
        for c in halo(1):
            c.wait_send()

    for i in range(1, NG):
        a_copy(i, a).wait_send()
        b_copy(i, (b + i) % NG, b).wait_send()
        gb_copy(i, oct_b).wait_send()
        ga_copy(i, oct_a).wait_send()

    def sent_z(i, _):
        z_copy(i, (z + i) % NZ, z).wait_send()
        gz_copy(i, oct_z).wait_send()
        return 0

    lax.fori_loop(1, NZ, sent_z, 0)
    gc_copy(core).wait_send()


OWN_AT = (4, 12)
NEAR_AT = (0, 2, 4, 7, 13)


def body(points, charges, leaf_density, leaf_octant, user_lists, near_leaves, near_codes,
         upward_map, lower_map, upper_map, downward_map):
    meta = jnp.concatenate(
        [leaf_octant, user_lists.reshape(-1), near_leaves.reshape(-1), near_codes.reshape(-1)]
    )
    vmem = pl.BlockSpec(memory_space=pltpu.VMEM)
    dma = pltpu.SemaphoreType.DMA
    n_oct = 2 * NX * NY * NZ
    return pl.pallas_call(
        kernel,
        out_shape=jax.ShapeDtypeStruct((LB, Q, PTS), F32),
        in_specs=[pl.BlockSpec(memory_space=pltpu.SMEM)] + [vmem] * 8,
        out_specs=vmem,
        scratch_shapes=[
            pltpu.VMEM((LB + 2, 8, PTS), F32),
            pltpu.VMEM((LB + 2 * UH, PTS, 48), BF16),
            pltpu.VMEM((LB + 2 * UH, 16, PTS), BF16),
            pltpu.VMEM((2, LB, 3, PTS), F32),
            pltpu.VMEM((2, LB, Q, PTS), F32),
            pltpu.VMEM((LB, 16, PTS), F32),
            pltpu.VMEM((2 * NG, ROWS + 8, SP), F32),
            pltpu.VMEM((NG * NZ * Q, SP), F32),
            pltpu.VMEM((NG, NZ * Q, SP), F32),
            pltpu.VMEM((NZ, Q, SP), F32),
            pltpu.VMEM((NZ, Q, SP), F32),
            pltpu.VMEM((n_oct, Q, SP), F32),
            pltpu.VMEM((2 * ROWS, SP), F32),
            pltpu.VMEM((LB // 2, 16, SP), BF16),
            dma((4,)), dma((4,)), dma, dma,
            dma((NG,)), dma((NG,)), dma((NG,)), dma((NG,)), dma((NZ,)), dma((NZ,)),
            dma((NZ,)), dma((NZ,)), dma((NG,)), dma((NG,)), dma((NG,)), dma((NG,)), dma, dma,
        ],
        compiler_params=pltpu.CompilerParams(
            collective_id=0, has_side_effects=True, vmem_limit_bytes=50 * 2**20
        ),
    )(
        meta, points, charges, leaf_density, upward_map, lower_map, upper_map, downward_map,
        jnp.asarray(surface_features()),
    )


def solution(mesh):
    in_specs = (
        P("cube", None, None),
        P("cube", None, None),
        P("cube", None, None),
        P("cube"),
        P("cube", None, None),
        P("cube", None),
        P("cube", None),
        P(),
        P(),
        P(),
        P(),
    )
    return jax.shard_map(
        body, mesh=mesh, in_specs=in_specs, out_specs=P("cube", None, None), check_vma=False
    )
```

time: 967 us -> 95.8 us (0.10)
  waiting for transfers between devices: 673 us -> 0 us
  matrix products: 141 us -> 0 us
  Pallas kernels: 0 us -> 86.6 us
  other arithmetic: 71.1 us -> 0.08 us
  local copies, waits for them, and re-layouts: 49.4 us -> 8.42 us
  starting transfers between devices: 17.3 us -> 0 us
  between operations: 13.7 us -> 0.07 us
    unnamed x3 -> x0, waiting for transfers between devices: 489 us -> none
    all_gather x1 -> x0, waiting for transfers between devices: 181 us -> none  [body(): shard_rows = lax.all_gather(owned_local, 'cube', axis=0, tiled=True)]
    dot_general x54 -> x0, matrix products: 141 us -> none  [the longest x32 111 us: block(): jnp.einsum('lps,lqs->lqp', kernel(targets, sources), set_charges[rows], p...]
    pallas_call x0 -> x1, Pallas kernels: none -> 86.6 us  [body(): pl.pallas_call(kernel, out_shape=jax.ShapeDtypeStruct((LB, Q, PTS), F32),...]
    reduce_sum x16 -> x0, other arithmetic: 66.4 us -> none  [kernel(): jnp.sum(separation * separation, axis=-3) + soften]
    gather x68 -> x0, local copies, waits for them, and re-layouts: 39.2 us -> none  [the longest x32 18.6 us: block(): set_charges[rows]]
    ppermute x6 -> x0, starting transfers between devices: 17.3 us -> none  [passed_along(): lax.ppermute(value, axis, [(source, source + steps) for source in range(i...]
  transfers between devices with their start and end apart: 8 -> 0, of which waited for: 4 -> 0; matrix products, arithmetic and copies ran while one was open for 0% -> 0% of each run, Pallas kernels for 0% -> 0%
where the time goes in v1:
time: 95.8 us; the launch traced here: 95.1 us
  Pallas kernels  86.6 us (90%)
  local copies, waits for them, and re-layouts  8.42 us (9%)
    pallas_call x1, Pallas kernels, body(): pl.pallas_call(kernel, out_shape=jax.ShapeDtypeStruct((LB, Q, PTS), F32),...  86.6 us
    unnamed x22, local copies, waits for them, and re-layouts  7.49 us

profile of v1, /device:TPU:1, one launch (start us, length us, event | category | flops | bytes accessed | tf_op | source)
XLA Modules:
  0.0 95.1 jit_solution(10221328655723920964)
XLA Ops:
  0.0 0.8 reshape.9
  0.8 0.0 copy-start.7
  0.8 0.0 copy-start.8
  0.8 0.8 copy.16
  1.5 0.0 copy-start.4
  1.6 0.1 reshape.10
  1.6 0.0 copy-done.7
  1.6 0.1 copy.17
  1.7 0.1 reshape.11
  1.8 0.0 copy-done.8
  1.8 0.1 pad_add_fusion.meta
  1.9 0.0 copy-start.5
  1.9 1.0 %copy.18.pts = f32[16,3,512]{2,1,0:T(4,128)S(1)} copy(f32[16,3,512]{2,0,1:T(8,128)} %param.12) | data formatting | bytes 196608 | tf_op args[0]
  2.9 0.0 copy-done.4
  2.9 0.0 copy-done.5
  2.9 0.0 copy-start
  2.9 1.0 %copy-done = f32[296,296]{1,0:T(8,128)S(1)} copy-done((f32[296,296]{1,0:T(8,128)S(1)}, f32[296,296]{1,0:T(8,128)}, u32[]{:S(2)}) %copy-start) | copy-done | bytes 350488
  4.0 0.0 copy-start.1
  4.0 1.0 %copy-done.1 = f32[296,296]{1,0:T(8,128)S(1)} copy-done((f32[296,296]{1,0:T(8,128)S(1)}, f32[296,296]{1,0:T(8,128)}, u32[]{:S(2)}) %copy-start.1) | copy-done | bytes 350488
  5.0 1.0 %copy-done.2 = f32[296,296]{1,0:T(8,128)S(1)} copy-done((f32[296,296]{1,0:T(8,128)S(1)}, f32[296,296]{1,0:T(8,128)}, u32[]{:S(2)}) %copy-start.2) | copy-done | bytes 350488
  6.0 1.0 %copy-done.3 = f32[296,296]{1,0:T(8,128)S(1)} copy-done((f32[296,296]{1,0:T(8,128)S(1)}, f32[296,296]{1,0:T(8,128)}, u32[]{:S(2)}) %copy-start.3) | copy-done | bytes 350488
  7.0 0.9 copy-done.6
  7.9 86.6 %shard_map.118 = f32[16,4,512]{2,1,0:T(4,128)S(1)} custom-call(s32[152]{0:T(256)S(1)} %pad_add_fusion.meta, f32[16,3,512]{2,1,0:T(4,128)S(1)} %copy.18.pts, f32[16,4,512]{2,1,0:T(4,128)S(1)} %copy-done.4, f32[16,4,296]{2,1,0:T(4,128)S(1)} %copy-done.5, f32[296,296]{1,0:T(8,128)S(1)} %copy-done, f32[296,296]{1,0:T(8,128)S(1)} %copy-done.1, ...), custom_call_target="tpu_custom_call" | custom-call | tf_op jit(solution)/shard_map/pallas_call | solution.py:429
  94.5 0.7 copy.20
  (3 shorter events, 0.0 us)
Async XLA Ops:
  0.8 0.9 copy-start.7
  0.8 1.1 %copy-start.8 = (s32[16]{0:T(128)S(1)}, s32[16]{0:T(128)}, u32[]{:S(2)}) copy-start(s32[16]{0:T(128)} %param.15) | copy-start | bytes 196
  1.5 1.4 %copy-start.4 = (f32[16,4,512]{2,1,0:T(4,128)S(1)}, f32[16,4,512]{2,1,0:T(4,128)}, u32[]{:S(2)}) copy-start(f32[16,4,512]{2,1,0:T(4,128)} %ch.1) | copy-start | bytes 393220
  1.9 1.0 %copy-start.5 = (f32[16,4,296]{2,1,0:T(4,128)S(1)}, f32[16,4,296]{2,1,0:T(4,128)}, u32[]{:S(2)}) copy-start(f32[16,4,296]{2,1,0:T(4,128)} %dens.1) | copy-start | bytes 227332
  2.9 1.0 %copy-start = (f32[296,296]{1,0:T(8,128)S(1)}, f32[296,296]{1,0:T(8,128)}, u32[]{:S(2)}) copy-start(f32[296,296]{1,0:T(8,128)} %up.1) | copy-start | bytes 1051396
  4.0 1.0 %copy-start.1 = (f32[296,296]{1,0:T(8,128)S(1)}, f32[296,296]{1,0:T(8,128)}, u32[]{:S(2)}) copy-start(f32[296,296]{1,0:T(8,128)} %low.1) | copy-start | bytes 1051396
  5.0 1.0 %copy-start.2 = (f32[296,296]{1,0:T(8,128)S(1)}, f32[296,296]{1,0:T(8,128)}, u32[]{:S(2)}) copy-start(f32[296,296]{1,0:T(8,128)} %upp.1) | copy-start | bytes 1051396
  6.0 1.0 %copy-start.3 = (f32[296,296]{1,0:T(8,128)S(1)}, f32[296,296]{1,0:T(8,128)}, u32[]{:S(2)}) copy-start(f32[296,296]{1,0:T(8,128)} %down.1) | copy-start | bytes 1051396
  7.0 0.9 copy-start.6

commit v2 on v1

v2 whole, which is shorter than its diff:
```python
import functools
import math

import jax
import jax.numpy as jnp
import numpy as np
from jax import lax
from jax.experimental import pallas as pl
from jax.experimental.pallas import tpu as pltpu
from jax.sharding import PartitionSpec as P

EQ_ORDER = 8
INV_FOUR_PI = 1.0 / (4.0 * math.pi)
SOFTEN = 0.01
LB = 16
UH = 4
K = 4
Q = 4
S = 296
SP = 384
PTS = 512
FAR = 304
ROWS = LB * Q
MESH = pl.DeviceIdType.MESH
F32 = jnp.float32
BF16 = jnp.bfloat16
NX, NY, NZ = 4, 4, 16
NG = 4


def surface_table():
    spacing = np.linspace(-1.0, 1.0, EQ_ORDER)
    mesh_x, mesh_y, mesh_z = np.meshgrid(spacing, spacing, spacing, indexing="ij")
    lattice = np.stack([mesh_x.ravel(), mesh_y.ravel(), mesh_z.ravel()], 0)
    on_boundary = np.max(np.abs(lattice), axis=0) > 0.999
    return lattice[:, on_boundary] * 2.95


def split3(v):
    a = v.astype(BF16).astype(F32)
    r = v - a
    b = r.astype(BF16).astype(F32)
    return a, b, r - b


def source_features(p, row):
    nsq = jnp.sum(p * p, axis=0, keepdims=True)
    u = jnp.where(row == 3, nsq, jnp.where(row == 4, 1.0, p))
    a, b, c = split3(u)
    return jnp.concatenate([a, a, b, b, a, c], axis=0)


def target_features(t, row):
    nsq = jnp.sum(t * t, axis=0, keepdims=True) + SOFTEN
    v = jnp.where(row == 3, 1.0, jnp.where(row == 4, nsq, -2.0 * t))
    a, b, c = split3(v)
    return jnp.concatenate([a, b, a, b, c, a], axis=0).astype(BF16)


def surface_features():
    pts = np.zeros((8, FAR), np.float32)
    pts[:3, :S] = surface_table().astype(np.float32)
    pts[:3, S:] = pts[:3, :1]
    u = pts.copy()
    u[3] = np.sum(pts * pts, axis=0)
    u[4] = 1.0
    a = u.astype(jnp.bfloat16).astype(np.float32)
    b = (u - a).astype(jnp.bfloat16).astype(np.float32)
    c = u - a - b
    return np.ascontiguousarray(np.concatenate([a, a, b, b, a, c], axis=0).T)


def green(feat, ft):
    g = lax.rsqrt(jnp.dot(feat, ft, preferred_element_type=F32))
    hi = g.astype(BF16)
    return hi, (g - hi.astype(F32)).astype(BF16)


def pair_sum(feat, ft, weights):
    parts = []
    for at in range(0, PTS, 256):
        hi, lo = green(feat, ft[:, at : at + 256])
        parts.append(
            jnp.dot(weights, hi, preferred_element_type=F32)
            + jnp.dot(weights, lo, preferred_element_type=F32)
        )
    return jnp.concatenate(parts, axis=1)


def split2(v):
    hi = v.astype(BF16)
    return hi, (v - hi.astype(F32)).astype(BF16)


def dot3(x, w_hi, w_lo):
    hi, lo = split2(x)
    n = x.shape[0]
    both = jnp.concatenate([hi, lo], axis=0)
    r = jnp.dot(both, w_hi, preferred_element_type=F32)
    return r[:n] + r[n:] + jnp.dot(hi, w_lo, preferred_element_type=F32)


def kernel(
    octs, users, nears, codes, pts_in, ch_in, dens_in, up_in, low_in, upp_in, down_in, surf_in,
    out,
    pts, ch, dens, maps, surf, maps_hi, maps_lo, fsurf,
    xp, fs, cw, hp, hc, near, rbuf, p1, qb, p2, zb, gz, g2, wb, sbuf, vbuf, tot, ebuf, cfar, gh, gl,
    near_s, far_s, load_s, halo_s, halo_r, core_s, core_r, am_s, am_r, ao_s, ao_r, b_s, b_r, z_s, z_r,
    gz_s, gz_r, gb_s, gb_r, v_s, v_r, e_s, e_r,
):
    me = lax.axis_index("cube")
    count = 2 * NX * NY * NZ
    core = me % 2
    z = (me // 2) % NZ
    y = (me // (2 * NZ)) % NY
    x = me // (2 * NZ * NY)
    stride_x, stride_y = 2 * NZ * NY, 2 * NZ
    stride_a = stride_x * (1 - core) + stride_y * core
    stride_b = stride_y * (1 - core) + stride_x * core
    a = x * (1 - core) + y * core
    b = y * (1 - core) + x * core
    a_partner = y * (1 - core) + x * core
    partner = me + 1 - 2 * core
    oct_a = core * (NG * NG * NZ) + a * (NG * NZ)

    def peer_a(i):
        return me + ((a + i) % NG - a) * stride_a

    def peer_b(i):
        return me + ((b + i) % NG - b) * stride_b

    def peer_z(i):
        return me + ((z + i) % NZ - z) * 2

    def send(src, dst, s, r, dev):
        return pltpu.make_async_remote_copy(
            src_ref=src, dst_ref=dst, send_sem=s, recv_sem=r, device_id=(dev,), device_id_type=MESH
        )

    row8 = lax.broadcasted_iota(jnp.int32, (8, PTS), 0)

    barrier = pltpu.get_barrier_semaphore()

    def greet(dev):
        pl.semaphore_signal(barrier, inc=1, device_id=(dev,), device_id_type=MESH)

    greet(partner)
    for i in range(1, NG):
        greet(peer_a(i))
        greet(peer_b(i))

    z_near = (1, 2, NZ - 2, NZ - 1) if NZ == 16 else tuple(range(1, NZ))
    for i in z_near:
        greet(peer_z(i))
    n_greet = 1 + 2 * (NG - 1) + len(z_near)

    def tell(sem, reach):
        if NZ == 16:
            for i in (reach, NZ - reach):
                pl.semaphore_signal(sem, inc=1, device_id=(peer_z(i),), device_id_type=MESH)

    def step_near():
        if NZ == 16:
            pl.semaphore_wait(near_s, 2)
        tell(far_s, 4)

    def step_far():
        if NZ == 16:
            pl.semaphore_wait(far_s, 2)

    @pl.when(me > 0)
    def _():
        greet(me - 1)

    @pl.when(me < count - 1)
    def _():
        greet(me + 1)

    def load(i):
        src = (dens_in, pts_in, ch_in, surf_in, up_in, low_in, upp_in, down_in)[i]
        dst = (dens, pts, ch, surf, maps.at[0], maps.at[1], maps.at[2], maps.at[3])[i]
        return pltpu.make_async_copy(src, dst, load_s.at[i])

    for i in range(8):
        load(i).start()

    mine = a * 2 + core
    lane = lax.broadcasted_iota(jnp.int32, (8, SP), 1) % ROWS
    tail_q = lax.broadcasted_iota(jnp.int32, (Q, SP - S), 0)
    keys = jnp.zeros((8, SP), jnp.int32)
    for l in range(LB):
        keys = jnp.where(lane // Q == l, octs[l], keys)
    rbuf[mine, ROWS : ROWS + 8, :] = (keys * Q + lane % Q).astype(F32)
    load(0).wait()
    for l in range(LB):
        rbuf[mine, Q * l : Q * l + Q, 0:S] = dens[l]
        rbuf[mine, Q * l : Q * l + Q, S:SP] = (tail_q + octs[l] * Q).astype(F32)

    n_wait = n_greet + (me + count - 1) // count + (2 * count - 2 - me) // count
    pl.semaphore_wait(barrier, n_wait)

    def halo(i):
        dev = me + 1 - 2 * i
        return (
            send(pts_in, hp.at[i], halo_s.at[i], halo_r.at[i], dev),
            send(ch_in, hc.at[i], halo_s.at[2 + i], halo_r.at[2 + i], dev),
        )

    core_out = send(rbuf.at[mine], rbuf.at[a_partner * 2 + core], core_s, core_r, partner)
    core_in = send(rbuf.at[mine], rbuf.at[a * 2 + 1 - core], core_s, core_r, partner)

    def row_copy(s, r, i, slot):
        return send(rbuf.at[slot], rbuf.at[slot], s.at[i], r.at[i], peer_a(i))

    def am_copy(i, at):
        return row_copy(am_s, am_r, i, at * 2 + core)

    def ao_copy(i, at):
        return row_copy(ao_s, ao_r, i, at * 2 + 1 - core)

    def b_copy(i, chunk, at):
        return send(p1.at[pl.ds(chunk * NZ * Q, NZ * Q)], qb.at[at], b_s.at[i], b_r.at[i], peer_b(i))

    def z_copy(i, chunk, at):
        return send(p2.at[chunk], zb.at[at], z_s.at[i], z_r.at[i], peer_z(i))

    def gz_copy(i, at):
        return send(gz.at[at], gz.at[at], gz_s.at[i], gz_r.at[i], peer_z(i))

    def gb_copy(i, at):
        return send(wb.at[at], wb.at[at], gb_s.at[i], gb_r.at[i], peer_b(i))

    def v_copy(i, chunk, at):
        return send(sbuf.at[pl.ds(chunk * 2, 2)], vbuf.at[at], v_s.at[i], v_r.at[i], peer_a(i))

    core_out.start()
    for i in range(1, NG):
        am_copy(i, a).start()
    tell(near_s, 2)

    @pl.when(me < count - 1)
    def _():
        for c in halo(0):
            c.start()

    @pl.when(me > 0)
    def _():
        for c in halo(1):
            c.start()

    def step_a():
        core_in.wait_recv()
        for i in range(1, NG):
            ao_copy(i, a).start()

    def step_b():
        for i in range(1, NG):
            am_copy(i, (a + NG - i) % NG).wait_recv()
            ao_copy(i, (a + NG - i) % NG).wait_recv()
        rows = lax.broadcasted_iota(jnp.int32, (NG * NZ * Q, 3 * ROWS), 0) + oct_a * Q
        rows = rows.astype(F32)

        def add(j, _):
            member = jnp.where(rows == rbuf[j, ROWS : ROWS + 1, 0 : 3 * ROWS], 1.0, 0.0).astype(BF16)
            parts = jnp.concatenate(split3(rbuf[j, 0:ROWS, :]), axis=0).astype(BF16)
            p1[...] += jnp.dot(member, parts, preferred_element_type=F32)
            return 0

        p1[...] = jnp.zeros(p1.shape, F32)
        lax.fori_loop(0, 2 * NG, add, 0)
        for i in range(1, NG):
            b_copy(i, (b + i) % NG, b).start()

    def step_z():
        total = p1[pl.ds(pl.multiple_of(b * NZ * Q, 8), NZ * Q), :]
        for i in range(1, NG):
            at = (b + NG - i) % NG
            b_copy(i, at, at).wait_recv()
            total = total + qb[at]
        for j in range(NZ):
            p2[j] = total[Q * j : Q * j + Q, :]

        def go(i, _):
            z_copy(i, (z + i) % NZ, z).start()
            return 0

        lax.fori_loop(1, NZ, go, 0)

    def step_gz():
        def take(i, total):
            at = (z + NZ - i) % NZ
            z_copy(i, at, at).wait_recv()
            return total + zb[at]

        gz[z] = lax.fori_loop(1, NZ, take, p2[z])

        def go(i, _):
            gz_copy(i, z).start()
            return 0

        lax.fori_loop(1, NZ, go, 0)

    def step_gb():
        def take(i, _):
            gz_copy(i, (z + NZ - i) % NZ).wait_recv()
            return 0

        lax.fori_loop(1, NZ, take, 0)
        for j in range(NZ):
            g2[Q * j : Q * j + Q, :] = gz[j]
        e = dot3(g2[:, 0:S], maps_hi[0], maps_lo[0])
        none = jnp.zeros((8, S), F32)
        w = jnp.concatenate([none, dot3(e, maps_hi[1], maps_lo[1])], axis=0) + jnp.concatenate(
            [dot3(e, maps_hi[2], maps_lo[2]), none], axis=0
        )
        wb[b] = jnp.zeros(wb.shape[1:], F32)
        wb[b, :, 0:S] = dot3(w, maps_hi[3], maps_lo[3]) * INV_FOUR_PI
        for i in range(1, NG):
            gb_copy(i, b).start()

    def step_v():
        for i in range(1, NG):
            gb_copy(i, (b + NG - i) % NG).wait_recv()
        ext = NZ * Q + 8
        cols = lax.broadcasted_iota(jnp.int32, (2 * ROWS, NG * ext), 1)
        cols = cols % ext + (cols // ext) * (NZ * Q) + (oct_a - 1) * Q
        cols = cols.astype(F32)
        hi, lo = split2(wb[...].reshape(NG * ext, SP))
        for i in list(range(1, NG)) + [0]:
            at = (a + i) % NG
            key = rbuf[pl.ds(at * 2, 2), 0:ROWS, S : S + 1].reshape(2 * ROWS, 1)
            member = jnp.where(cols == key, 1.0, 0.0).astype(BF16)
            picked = jnp.dot(member, hi, preferred_element_type=F32) + jnp.dot(
                member, lo, preferred_element_type=F32
            )
            sbuf[pl.ds(at * 2, 2)] = picked.reshape(2, ROWS, SP)
            if i > 0:
                v_copy(i, at, a).start()

    def e_copy(c):
        return send(tot.at[c], ebuf, e_s, e_r, partner)

    def step_e():
        total = sbuf[pl.ds(a * 2, 2)]
        for i in range(1, NG):
            at = (a + NG - i) % NG
            v_copy(i, at, at).wait_recv()
            total = total + vbuf[at]
        tot[...] = total
        e_copy(1 - core).start()

    steps = (step_a, step_near, step_far, step_b, step_z, step_gz, step_gb, step_v, step_e)

    def run_steps(at):
        for place, step in zip(STEP_AT, steps):

            @pl.when(at == place)
            def _():
                step()

    def prep(n, p, q):
        fs[n] = source_features(p, row8).T.astype(BF16)
        hi = q.astype(BF16).astype(F32)
        lo = q - hi
        cw[n] = jnp.concatenate([hi + pltpu.roll(lo, 4, 0), jnp.zeros((8, PTS), F32)], axis=0).astype(BF16)

    xp[...] = jnp.zeros(xp.shape, F32)
    load(1).wait()
    load(2).wait()

    def prep_own(n, _):
        for c in range(3):
            xp[n, c : c + 1, :] = pts[c, pl.ds(n, 1), :]
        xp[LB, 0:4, :] = ch[n] * INV_FOUR_PI
        prep(n, xp[n], xp[LB])
        return 0

    lax.fori_loop(0, LB, prep_own, 0)
    for i in range(3, 8):
        load(i).wait()
    fsurf[...] = surf[...].astype(BF16)
    for i in range(4):
        maps_hi[i], maps_lo[i] = split2(maps[i])

    def own_pair(t, _):
        for h in range(2):
            l = 2 * t + h
            near[l] = pair_sum(fs[l], target_features(xp[l], row8), cw[l])
        run_steps(2 * t)
        return 0

    lax.fori_loop(0, LB // 2, own_pair, 0)

    for i in range(2):
        present = me > 0 if i == 0 else me < count - 1

        @pl.when(present)
        def _():
            for c in halo(i):
                c.wait_recv()

        @pl.when(jnp.logical_not(present))
        def _():
            hp[i] = jnp.zeros(hp.shape[1:], F32)
            hc[i] = jnp.zeros(hc.shape[1:], F32)

    for i in range(2):

        def prep_halo(j, _):
            n = users[i, j]
            for c in range(3):
                xp[LB + 1, c : c + 1, :] = hp[i, c, pl.ds(n, 1), :]
            xp[LB, 0:4, :] = hc[i, n] * INV_FOUR_PI
            prep(LB + i * UH + j, xp[LB + 1], xp[LB])
            return 0

        lax.fori_loop(0, UH, prep_halo, 0)

    def near_leaf(l, _):
        acc = near[l]
        box = xp[l]
        for k in range(K):
            n = nears[k, l]
            code = codes[k, l]
            code = jnp.where(code >= 13, code + 1, code)
            ox = (2 * (code // 9 - 1)).astype(F32)
            oy = (2 * ((code // 3) % 3 - 1)).astype(F32)
            oz = (2 * (code % 3 - 1)).astype(F32)
            off = jnp.where(row8 == 0, ox, jnp.where(row8 == 1, oy, jnp.where(row8 == 2, oz, 0.0)))
            acc = acc + pair_sum(fs[n], target_features(box - off, row8), cw[n])
        near[l] = acc
        run_steps(LB + l)
        return 0

    lax.fori_loop(0, LB, near_leaf, 0)

    def far_leaf(l, _):
        gh[l], gl[l] = green(fsurf[...], target_features(xp[l], row8))
        run_steps(2 * LB + l)
        return 0

    lax.fori_loop(0, LB, far_leaf, 0)

    e_copy(core).wait_recv()
    w = tot[core] + ebuf[...]
    hi = w.astype(BF16).astype(F32)
    lo = w - hi
    for t in range(LB // 2):
        pair = jnp.concatenate([hi[8 * t : 8 * t + 8], lo[8 * t : 8 * t + 8]], axis=0)
        cfar[t] = pair.astype(BF16)

    def far_pair(t, _):
        for h in range(2):
            l = 2 * t + h
            c = cfar[t, :, 0:FAR]
            far = jnp.dot(c, gh[l], preferred_element_type=F32) + jnp.dot(
                c, gl[l], preferred_element_type=F32
            )
            far = far[0:8] + far[8:16]
            out[l] = far[4 * h : 4 * h + 4] + near[l, 0:4, :] + near[l, 4:8, :]
        return 0

    lax.fori_loop(0, LB // 2, far_pair, 0)

    core_out.wait_send()

    @pl.when(me < count - 1)
    def _():
        for c in halo(0):
            c.wait_send()

    @pl.when(me > 0)
    def _():
        for c in halo(1):
            c.wait_send()

    for i in range(1, NG):
        am_copy(i, a).wait_send()
        ao_copy(i, a).wait_send()
        b_copy(i, (b + i) % NG, b).wait_send()
        gb_copy(i, b).wait_send()
        v_copy(i, (a + i) % NG, a).wait_send()

    def sent_z(i, _):
        z_copy(i, (z + i) % NZ, z).wait_send()
        gz_copy(i, z).wait_send()
        return 0

    lax.fori_loop(1, NZ, sent_z, 0)
    e_copy(1 - core).wait_send()


STEP_AT = (0, 6, 12, 8, 14, 19, 23, 27, 32)


def body(points, charges, leaf_density, leaf_octant, user_lists, near_leaves, near_codes,
         upward_map, lower_map, upper_map, downward_map):
    smem = pl.BlockSpec(memory_space=pltpu.SMEM)
    hbm = pl.BlockSpec(memory_space=pltpu.HBM)
    dma = pltpu.SemaphoreType.DMA
    return pl.pallas_call(
        kernel,
        out_shape=jax.ShapeDtypeStruct((LB, Q, PTS), F32),
        in_specs=[smem] * 4 + [hbm] * 8,
        out_specs=pl.BlockSpec(memory_space=pltpu.VMEM),
        scratch_shapes=[
            pltpu.VMEM((3, LB, PTS), F32),
            pltpu.VMEM((LB, Q, PTS), F32),
            pltpu.VMEM((LB, Q, S), F32),
            pltpu.VMEM((4, S, S), F32),
            pltpu.VMEM((FAR, 48), F32),
            pltpu.VMEM((4, S, S), BF16),
            pltpu.VMEM((4, S, S), BF16),
            pltpu.VMEM((FAR, 48), BF16),
            pltpu.VMEM((LB + 2, 8, PTS), F32),
            pltpu.VMEM((LB + 2 * UH, PTS, 48), BF16),
            pltpu.VMEM((LB + 2 * UH, 16, PTS), BF16),
            pltpu.VMEM((2, 3, LB, PTS), F32),
            pltpu.VMEM((2, LB, Q, PTS), F32),
            pltpu.VMEM((LB, 16, PTS), F32),
            pltpu.VMEM((2 * NG, ROWS + 8, SP), F32),
            pltpu.VMEM((NG * NZ * Q, SP), F32),
            pltpu.VMEM((NG, NZ * Q, SP), F32),
            pltpu.VMEM((NZ, Q, SP), F32),
            pltpu.VMEM((NZ, Q, SP), F32),
            pltpu.VMEM((NZ, Q, SP), F32),
            pltpu.VMEM((NZ * Q, SP), F32),
            pltpu.VMEM((NG, NZ * Q + 8, SP), F32),
            pltpu.VMEM((2 * NG, ROWS, SP), F32),
            pltpu.VMEM((NG, 2, ROWS, SP), F32),
            pltpu.VMEM((2, ROWS, SP), F32),
            pltpu.VMEM((ROWS, SP), F32),
            pltpu.VMEM((LB // 2, 16, SP), BF16),
            pltpu.VMEM((LB, FAR, PTS), BF16),
            pltpu.VMEM((LB, FAR, PTS), BF16),
            pltpu.SemaphoreType.REGULAR, pltpu.SemaphoreType.REGULAR,
            dma((8,)), dma((4,)), dma((4,)), dma, dma,
            dma((NG,)), dma((NG,)), dma((NG,)), dma((NG,)),
            dma((NG,)), dma((NG,)), dma((NZ,)), dma((NZ,)), dma((NZ,)), dma((NZ,)),
            dma((NG,)), dma((NG,)), dma((NG,)), dma((NG,)), dma, dma,
        ],
        compiler_params=pltpu.CompilerParams(
            collective_id=0, has_side_effects=True, vmem_limit_bytes=56 * 2**20
        ),
    )(
        leaf_octant, user_lists.reshape(2, UH), near_leaves.T, near_codes.T,
        points.transpose(1, 0, 2), charges, leaf_density,
        upward_map, lower_map, upper_map, downward_map, jnp.asarray(surface_features(), F32),
    )


def solution(mesh):
    in_specs = (
        P("cube", None, None),
        P("cube", None, None),
        P("cube", None, None),
        P("cube"),
        P("cube", None, None),
        P("cube", None),
        P("cube", None),
        P(),
        P(),
        P(),
        P(),
    )
    return jax.shard_map(
        body, mesh=mesh, in_specs=in_specs, out_specs=P("cube", None, None), check_vma=False
    )
```

time: 95.8 us -> 75 us (0.78)
  the two profiles are of different devices: /device:TPU:1 before, /device:TPU:4 now
where the time goes in v2:
time: 75 us; the launch traced here: 74.8 us
  Pallas kernels  73.2 us (98%)
  local copies, waits for them, and re-layouts  1.57 us (2%)
    pallas_call x1, Pallas kernels, body(): pl.pallas_call(kernel, out_shape=jax.ShapeDtypeStruct((LB, Q, PTS), F32),...  73.2 us
    unnamed x1, local copies, waits for them, and re-layouts  1.57 us

profile of v2, /device:TPU:4, one launch (start us, length us, event | category | flops | bytes accessed | tf_op | source)
XLA Modules:
  0.0 74.8 jit_solution(17655877715065676814)
XLA Ops:
  0.0 73.2 %shard_map.118 = f32[16,4,512]{2,1,0:T(4,128)} custom-call(s32[16]{0:T(128)} %octs.1, s32[2,4]{1,0:T(2,128)} %bitcast.7, s32[4,16]{1,0:T(4,128)} %bitcast.5, s32[4,16]{1,0:T(4,128)} %bitcast.6, f32[3,16,512]{2,1,0:T(8,128)} %bitcast.4, f32[16,4,512]{2,1,0:T(4,128)} %ch_in.1, f32[16,4,296]{2,1,0:T(4,128)} %dens_in.1, f32[296,296]{1,0:T(8,128)} %up_in.1, ...), custom_call_target="tpu_custom_call" | custom-call | tf_op jit(solution)/shard_map/pallas_call | solution.py:501
  73.2 1.6 %copy.14 = f32[16,4,512]{2,1,0:T(4,128)} copy(f32[16,4,512]{2,1,0:T(4,128)} %shard_map.118) | data formatting | bytes 262144

commit v3 on v2

--- a/solution.py
+++ b/solution.py
@@ -104,9 +104,9 @@
     octs, users, nears, codes, pts_in, ch_in, dens_in, up_in, low_in, upp_in, down_in, surf_in,
     out,
     pts, ch, dens, maps, surf, maps_hi, maps_lo, fsurf,
-    xp, fs, cw, hp, hc, near, rbuf, p1, qb, p2, zb, gz, g2, wb, sbuf, vbuf, tot, ebuf, cfar, gh, gl,
-    near_s, far_s, load_s, halo_s, halo_r, core_s, core_r, am_s, am_r, ao_s, ao_r, b_s, b_r, z_s, z_r,
-    gz_s, gz_r, gb_s, gb_r, v_s, v_r, e_s, e_r,
+    xp, fs, cw, hp, hc, near, rbuf, p1, qb, p2, zb, gz, g2, wb, sbuf, vbuf, cfar, gh, gl,
+    near_s, far_s, load_s, halo_s, halo_r, a_s, a_r, b_s, b_r, z_s, z_r,
+    gz_s, gz_r, gb_s, gb_r, v_s, v_r,
 ):
     me = lax.axis_index("cube")
     count = 2 * NX * NY * NZ
@@ -119,7 +119,6 @@
     stride_b = stride_y * (1 - core) + stride_x * core
     a = x * (1 - core) + y * core
     b = y * (1 - core) + x * core
-    a_partner = y * (1 - core) + x * core
     partner = me + 1 - 2 * core
     oct_a = core * (NG * NG * NZ) + a * (NG * NZ)
 
@@ -131,6 +130,15 @@
 
     def peer_z(i):
         return me + ((z + i) % NZ - z) * 2
+
+    def cross_a(i):
+        return peer_a(i) + 1 - 2 * core
+
+    def cross_b(i):
+        return peer_b(i) + 1 - 2 * core
+
+    def far_first(t):
+        return NZ // 2 + (t + 1) // 2 * (1 - 2 * (t % 2))
 
     def send(src, dst, s, r, dev):
         return pltpu.make_async_remote_copy(
@@ -148,11 +156,13 @@
     for i in range(1, NG):
         greet(peer_a(i))
         greet(peer_b(i))
+        greet(cross_a(i))
+        greet(cross_b(i))
 
     z_near = (1, 2, NZ - 2, NZ - 1) if NZ == 16 else tuple(range(1, NZ))
     for i in z_near:
         greet(peer_z(i))
-    n_greet = 1 + 2 * (NG - 1) + len(z_near)
+    n_greet = 1 + 4 * (NG - 1) + len(z_near)
 
     def tell(sem, reach):
         if NZ == 16:
@@ -206,17 +216,17 @@
             send(ch_in, hc.at[i], halo_s.at[2 + i], halo_r.at[2 + i], dev),
         )
 
-    core_out = send(rbuf.at[mine], rbuf.at[a_partner * 2 + core], core_s, core_r, partner)
-    core_in = send(rbuf.at[mine], rbuf.at[a * 2 + 1 - core], core_s, core_r, partner)
-
-    def row_copy(s, r, i, slot):
-        return send(rbuf.at[slot], rbuf.at[slot], s.at[i], r.at[i], peer_a(i))
-
-    def am_copy(i, at):
-        return row_copy(am_s, am_r, i, at * 2 + core)
-
-    def ao_copy(i, at):
-        return row_copy(ao_s, ao_r, i, at * 2 + 1 - core)
+    def a_copy(i, slot):
+        dev = peer_a(i) if i < NG else cross_b(i - NG)
+        return send(rbuf.at[mine], rbuf.at[slot], a_s.at[i], a_r.at[i], dev)
+
+    def a_send(i):
+        return a_copy(i, mine if i < NG else b * 2 + core)
+
+    def a_take(i):
+        return a_copy(i, (a + 2 * NG - i) % NG * 2 + (core if i < NG else 1 - core))
+
+    a_all = tuple(range(1, 2 * NG))
 
     def b_copy(i, chunk, at):
         return send(p1.at[pl.ds(chunk * NZ * Q, NZ * Q)], qb.at[at], b_s.at[i], b_r.at[i], peer_b(i))
@@ -230,12 +240,19 @@
     def gb_copy(i, at):
         return send(wb.at[at], wb.at[at], gb_s.at[i], gb_r.at[i], peer_b(i))
 
-    def v_copy(i, chunk, at):
-        return send(sbuf.at[pl.ds(chunk * 2, 2)], vbuf.at[at], v_s.at[i], v_r.at[i], peer_a(i))
-
-    core_out.start()
-    for i in range(1, NG):
-        am_copy(i, a).start()
+    def v_copy(i, at):
+        dev = peer_a(i) if i < NG else cross_a(i - NG)
+        slot = (a + i) % NG * 2 + (core if i < NG else 1 - core)
+        return send(sbuf.at[slot], vbuf.at[at], v_s.at[i], v_r.at[i], dev)
+
+    def v_send(i):
+        return v_copy(i, a if i < NG else NG + a)
+
+    def v_place(i):
+        return (a + NG - i) % NG if i < NG else NG + (b + 2 * NG - i) % NG
+
+    for i in a_all:
+        a_send(i).start()
     tell(near_s, 2)
 
     @pl.when(me < count - 1)
@@ -248,15 +265,9 @@
         for c in halo(1):
             c.start()
 
-    def step_a():
-        core_in.wait_recv()
-        for i in range(1, NG):
-            ao_copy(i, a).start()
-
     def step_b():
-        for i in range(1, NG):
-            am_copy(i, (a + NG - i) % NG).wait_recv()
-            ao_copy(i, (a + NG - i) % NG).wait_recv()
+        for i in a_all:
+            a_take(i).wait_recv()
         rows = lax.broadcasted_iota(jnp.int32, (NG * NZ * Q, 3 * ROWS), 0) + oct_a * Q
         rows = rows.astype(F32)
 
@@ -280,11 +291,12 @@
         for j in range(NZ):
             p2[j] = total[Q * j : Q * j + Q, :]
 
-        def go(i, _):
+        def go(t, _):
+            i = far_first(t)
             z_copy(i, (z + i) % NZ, z).start()
             return 0
 
-        lax.fori_loop(1, NZ, go, 0)
+        lax.fori_loop(0, NZ - 1, go, 0)
 
     def step_gz():
         def take(i, total):
@@ -294,11 +306,11 @@
 
         gz[z] = lax.fori_loop(1, NZ, take, p2[z])
 
-        def go(i, _):
-            gz_copy(i, z).start()
+        def go(t, _):
+            gz_copy(far_first(t), z).start()
             return 0
 
-        lax.fori_loop(1, NZ, go, 0)
+        lax.fori_loop(0, NZ - 1, go, 0)
 
     def step_gb():
         def take(i, _):
@@ -335,21 +347,10 @@
             )
             sbuf[pl.ds(at * 2, 2)] = picked.reshape(2, ROWS, SP)
             if i > 0:
-                v_copy(i, at, a).start()
-
-    def e_copy(c):
-        return send(tot.at[c], ebuf, e_s, e_r, partner)
-
-    def step_e():
-        total = sbuf[pl.ds(a * 2, 2)]
-        for i in range(1, NG):
-            at = (a + NG - i) % NG
-            v_copy(i, at, at).wait_recv()
-            total = total + vbuf[at]
-        tot[...] = total
-        e_copy(1 - core).start()
-
-    steps = (step_a, step_near, step_far, step_b, step_z, step_gz, step_gb, step_v, step_e)
+                v_send(i).start()
+            v_send(NG + i).start()
+
+    steps = (step_near, step_far, step_b, step_z, step_gz, step_gb, step_v)
 
     def run_steps(at):
         for place, step in zip(STEP_AT, steps):
@@ -441,8 +442,10 @@
 
     lax.fori_loop(0, LB, far_leaf, 0)
 
-    e_copy(core).wait_recv()
-    w = tot[core] + ebuf[...]
+    w = sbuf[mine]
+    for i in a_all:
+        v_copy(i, v_place(i)).wait_recv()
+        w = w + vbuf[v_place(i)]
     hi = w.astype(BF16).astype(F32)
     lo = w - hi
     for t in range(LB // 2):
@@ -462,7 +465,9 @@
 
     lax.fori_loop(0, LB // 2, far_pair, 0)
 
-    core_out.wait_send()
+    for i in a_all:
+        a_send(i).wait_send()
+        v_send(i).wait_send()
 
     @pl.when(me < count - 1)
     def _():
@@ -475,11 +480,8 @@
             c.wait_send()
 
     for i in range(1, NG):
-        am_copy(i, a).wait_send()
-        ao_copy(i, a).wait_send()
         b_copy(i, (b + i) % NG, b).wait_send()
         gb_copy(i, b).wait_send()
-        v_copy(i, (a + i) % NG, a).wait_send()
 
     def sent_z(i, _):
         z_copy(i, (z + i) % NZ, z).wait_send()
@@ -487,10 +489,9 @@
         return 0
 
     lax.fori_loop(1, NZ, sent_z, 0)
-    e_copy(1 - core).wait_send()
-
-
-STEP_AT = (0, 6, 12, 8, 14, 19, 23, 27, 32)
+
+
+STEP_AT = (0, 6, 14, 17, 23, 28, 36)
 
 
 def body(points, charges, leaf_density, leaf_octant, user_lists, near_leaves, near_codes,
@@ -527,17 +528,14 @@
             pltpu.VMEM((NZ * Q, SP), F32),
             pltpu.VMEM((NG, NZ * Q + 8, SP), F32),
             pltpu.VMEM((2 * NG, ROWS, SP), F32),
-            pltpu.VMEM((NG, 2, ROWS, SP), F32),
-            pltpu.VMEM((2, ROWS, SP), F32),
-            pltpu.VMEM((ROWS, SP), F32),
+            pltpu.VMEM((2 * NG, ROWS, SP), F32),
             pltpu.VMEM((LB // 2, 16, SP), BF16),
             pltpu.VMEM((LB, FAR, PTS), BF16),
             pltpu.VMEM((LB, FAR, PTS), BF16),
             pltpu.SemaphoreType.REGULAR, pltpu.SemaphoreType.REGULAR,
-            dma((8,)), dma((4,)), dma((4,)), dma, dma,
-            dma((NG,)), dma((NG,)), dma((NG,)), dma((NG,)),
+            dma((8,)), dma((4,)), dma((4,)), dma((2 * NG,)), dma((2 * NG,)),
             dma((NG,)), dma((NG,)), dma((NZ,)), dma((NZ,)), dma((NZ,)), dma((NZ,)),
-            dma((NG,)), dma((NG,)), dma((NG,)), dma((NG,)), dma, dma,
+            dma((NG,)), dma((NG,)), dma((2 * NG,)), dma((2 * NG,)),
         ],
         compiler_params=pltpu.CompilerParams(
             collective_id=0, has_side_effects=True, vmem_limit_bytes=56 * 2**20

time: 75 us -> 70.3 us (0.937)
  the two profiles are of different devices: /device:TPU:4 before, /device:TPU:1 now
where the time goes in v3:
time: 70.3 us; the launch traced here: 70.2 us
  Pallas kernels  68.6 us (98%)
  local copies, waits for them, and re-layouts  1.57 us (2%)
    pallas_call x1, Pallas kernels, body(): pl.pallas_call(kernel, out_shape=jax.ShapeDtypeStruct((LB, Q, PTS), F32),...  68.6 us
    unnamed x1, local copies, waits for them, and re-layouts  1.57 us

profile of v3, /device:TPU:1, one launch (start us, length us, event | category | flops | bytes accessed | tf_op | source)
XLA Modules:
  0.0 70.2 jit_solution(14603036691376624337)
XLA Ops:
  0.0 68.6 %shard_map.118 = f32[16,4,512]{2,1,0:T(4,128)} custom-call(s32[16]{0:T(128)} %octs.1, s32[2,4]{1,0:T(2,128)} %bitcast.7, s32[4,16]{1,0:T(4,128)} %bitcast.5, s32[4,16]{1,0:T(4,128)} %bitcast.6, f32[3,16,512]{2,1,0:T(8,128)} %bitcast.4, f32[16,4,512]{2,1,0:T(4,128)} %ch_in.1, f32[16,4,296]{2,1,0:T(4,128)} %dens_in.1, f32[296,296]{1,0:T(8,128)} %up_in.1, ...), custom_call_target="tpu_custom_call" | custom-call | tf_op jit(solution)/shard_map/pallas_call | solution.py:502
  68.6 1.6 %copy.14 = f32[16,4,512]{2,1,0:T(4,128)} copy(f32[16,4,512]{2,1,0:T(4,128)} %shard_map.118) | data formatting | bytes 262144

commit v4 on v3

--- a/solution.py
+++ b/solution.py
@@ -21,6 +21,8 @@
 PTS = 512
 FAR = 304
 ROWS = LB * Q
+TAIL = S - 256
+PACKED = 2 * ROWS + 24
 MESH = pl.DeviceIdType.MESH
 F32 = jnp.float32
 BF16 = jnp.bfloat16
@@ -85,6 +87,25 @@
             + jnp.dot(weights, lo, preferred_element_type=F32)
         )
     return jnp.concatenate(parts, axis=1)
+
+
+def lane_of(shape):
+    return lax.broadcasted_iota(jnp.int32, shape, 1)
+
+
+def pack(v):
+    end = v[:, 256:SP]
+    last = jnp.concatenate([end[48:ROWS], jnp.zeros((8, 128), F32)], axis=0)
+    shared = end[0:24] + pltpu.roll(end[24:48], TAIL, 1) + pltpu.roll(last, 2 * TAIL, 1)
+    return jnp.concatenate([v[:, 0:128], v[:, 128:256], shared], axis=0)
+
+
+def unpack(p):
+    shared = p[2 * ROWS : PACKED]
+    keep = lane_of((24, 128)) < TAIL
+    ends = [jnp.where(keep, pltpu.roll(shared, (128 - TAIL * g) % 128, 1) if g else shared, 0.0) for g in range(3)]
+    end = jnp.concatenate([ends[0], ends[1], ends[2][0:16]], axis=0)
+    return jnp.concatenate([p[0:ROWS], p[ROWS : 2 * ROWS], end], axis=1)
 
 
 def split2(v):
@@ -195,16 +216,41 @@
         load(i).start()
 
     mine = a * 2 + core
-    lane = lax.broadcasted_iota(jnp.int32, (8, SP), 1) % ROWS
-    tail_q = lax.broadcasted_iota(jnp.int32, (Q, SP - S), 0)
-    keys = jnp.zeros((8, SP), jnp.int32)
+    lane = lane_of((8, 128)) % ROWS
+    keys = jnp.zeros((8, 128), jnp.int32)
     for l in range(LB):
         keys = jnp.where(lane // Q == l, octs[l], keys)
-    rbuf[mine, ROWS : ROWS + 8, :] = (keys * Q + lane % Q).astype(F32)
+    rbuf[mine, PACKED : PACKED + 8, :] = (keys * Q + lane % Q).astype(F32)
+    row24 = lax.broadcasted_iota(jnp.int32, (24, 128), 0)
+    lane24 = lane_of((24, 128))
+    column = jnp.zeros((24, 128), jnp.int32)
+    for l in range(LB):
+        here = jnp.logical_and(row24 // Q == l % 6, lane24 == 3 * TAIL + l // 6)
+        column = jnp.where(here, octs[l] * Q + row24 % Q, column)
+    g2[...] = jnp.zeros(g2.shape, F32)
     load(0).wait()
     for l in range(LB):
-        rbuf[mine, Q * l : Q * l + Q, 0:S] = dens[l]
-        rbuf[mine, Q * l : Q * l + Q, S:SP] = (tail_q + octs[l] * Q).astype(F32)
+        g2[Q * l : Q * l + Q, 0:S] = dens[l]
+    packed = pack(g2[0:ROWS])
+    rbuf[mine, 0 : 2 * ROWS, :] = packed[0 : 2 * ROWS]
+    rbuf[mine, 2 * ROWS : PACKED, :] = packed[2 * ROWS : PACKED] + column.astype(F32)
+
+    def prep(n, p, q):
+        fs[n] = source_features(p, row8).T.astype(BF16)
+        hi = q.astype(BF16).astype(F32)
+        cw[n] = jnp.concatenate([hi, q - hi, jnp.zeros((8, PTS), F32)], axis=0).astype(BF16)
+
+    xp[...] = jnp.zeros(xp.shape, F32)
+    load(1).wait()
+    load(2).wait()
+
+    def prep_own(n, _):
+        for c in range(3):
+            xp[n, c : c + 1, :] = pts[c, pl.ds(n, 1), :]
+        prep(n, xp[n], ch[n] * INV_FOUR_PI)
+        return 0
+
+    lax.fori_loop(0, LB // 2, prep_own, 0, unroll=2)
 
     n_wait = n_greet + (me + count - 1) // count + (2 * count - 2 - me) // count
     pl.semaphore_wait(barrier, n_wait)
@@ -272,8 +318,10 @@
         rows = rows.astype(F32)
 
         def add(j, _):
-            member = jnp.where(rows == rbuf[j, ROWS : ROWS + 1, 0 : 3 * ROWS], 1.0, 0.0).astype(BF16)
-            parts = jnp.concatenate(split3(rbuf[j, 0:ROWS, :]), axis=0).astype(BF16)
+            key = rbuf[j, PACKED : PACKED + 1, :]
+            key = jnp.concatenate([key, key[:, 0:ROWS]], axis=1)
+            member = jnp.where(rows == key, 1.0, 0.0).astype(BF16)
+            parts = jnp.concatenate(split3(unpack(rbuf[j, 0:PACKED, :])), axis=0).astype(BF16)
             p1[...] += jnp.dot(member, parts, preferred_element_type=F32)
             return 0
 
@@ -320,7 +368,7 @@
         lax.fori_loop(1, NZ, take, 0)
         for j in range(NZ):
             g2[Q * j : Q * j + Q, :] = gz[j]
-        e = dot3(g2[:, 0:S], maps_hi[0], maps_lo[0])
+        e = dot3(g2[0 : NZ * Q, 0:S], maps_hi[0], maps_lo[0])
         none = jnp.zeros((8, S), F32)
         w = jnp.concatenate([none, dot3(e, maps_hi[1], maps_lo[1])], axis=0) + jnp.concatenate(
             [dot3(e, maps_hi[2], maps_lo[2]), none], axis=0
@@ -340,12 +388,18 @@
         hi, lo = split2(wb[...].reshape(NG * ext, SP))
         for i in list(range(1, NG)) + [0]:
             at = (a + i) % NG
-            key = rbuf[pl.ds(at * 2, 2), 0:ROWS, S : S + 1].reshape(2 * ROWS, 1)
+            key = []
+            for h in range(2):
+                shared = rbuf[at * 2 + h, 2 * ROWS : PACKED, :]
+                for g, n in enumerate((24, 24, 16)):
+                    key.append(shared[0:n, 3 * TAIL + g : 3 * TAIL + g + 1])
+            key = jnp.concatenate(key, axis=0)
             member = jnp.where(cols == key, 1.0, 0.0).astype(BF16)
             picked = jnp.dot(member, hi, preferred_element_type=F32) + jnp.dot(
                 member, lo, preferred_element_type=F32
             )
-            sbuf[pl.ds(at * 2, 2)] = picked.reshape(2, ROWS, SP)
+            for h in range(2):
+                sbuf[at * 2 + h] = pack(picked[h * ROWS : h * ROWS + ROWS])
             if i > 0:
                 v_send(i).start()
             v_send(NG + i).start()
@@ -359,24 +413,7 @@
             def _():
                 step()
 
-    def prep(n, p, q):
-        fs[n] = source_features(p, row8).T.astype(BF16)
-        hi = q.astype(BF16).astype(F32)
-        lo = q - hi
-        cw[n] = jnp.concatenate([hi + pltpu.roll(lo, 4, 0), jnp.zeros((8, PTS), F32)], axis=0).astype(BF16)
-
-    xp[...] = jnp.zeros(xp.shape, F32)
-    load(1).wait()
-    load(2).wait()
-
-    def prep_own(n, _):
-        for c in range(3):
-            xp[n, c : c + 1, :] = pts[c, pl.ds(n, 1), :]
-        xp[LB, 0:4, :] = ch[n] * INV_FOUR_PI
-        prep(n, xp[n], xp[LB])
-        return 0
-
-    lax.fori_loop(0, LB, prep_own, 0)
+    lax.fori_loop(LB // 2, LB, prep_own, 0, unroll=2)
     for i in range(3, 8):
         load(i).wait()
     fsurf[...] = surf[...].astype(BF16)
@@ -409,13 +446,13 @@
 
         def prep_halo(j, _):
             n = users[i, j]
+            at = LB + i * UH + j
             for c in range(3):
-                xp[LB + 1, c : c + 1, :] = hp[i, c, pl.ds(n, 1), :]
-            xp[LB, 0:4, :] = hc[i, n] * INV_FOUR_PI
-            prep(LB + i * UH + j, xp[LB + 1], xp[LB])
+                xp[at, c : c + 1, :] = hp[i, c, pl.ds(n, 1), :]
+            prep(at, xp[at], hc[i, n] * INV_FOUR_PI)
             return 0
 
-        lax.fori_loop(0, UH, prep_halo, 0)
+        lax.fori_loop(0, UH, prep_halo, 0, unroll=2)
 
     def near_leaf(l, _):
         acc = near[l]
@@ -435,17 +472,20 @@
 
     lax.fori_loop(0, LB, near_leaf, 0)
 
-    def far_leaf(l, _):
-        gh[l], gl[l] = green(fsurf[...], target_features(xp[l], row8))
-        run_steps(2 * LB + l)
+    def far_some(t, _):
+        for h in range(4):
+            l = 4 * t + h
+            gh[l], gl[l] = green(fsurf[...], target_features(xp[l], row8))
+        run_steps(2 * LB + 4 * t)
         return 0
 
-    lax.fori_loop(0, LB, far_leaf, 0)
+    lax.fori_loop(0, LB // 4, far_some, 0)
 
     w = sbuf[mine]
     for i in a_all:
         v_copy(i, v_place(i)).wait_recv()
         w = w + vbuf[v_place(i)]
+    w = unpack(w)
     hi = w.astype(BF16).astype(F32)
     lo = w - hi
     for t in range(LB // 2):
@@ -463,7 +503,7 @@
             out[l] = far[4 * h : 4 * h + 4] + near[l, 0:4, :] + near[l, 4:8, :]
         return 0
 
-    lax.fori_loop(0, LB // 2, far_pair, 0)
+    lax.fori_loop(0, LB // 2, far_pair, 0, unroll=2)
 
     for i in a_all:
         a_send(i).wait_send()
@@ -491,7 +531,7 @@
     lax.fori_loop(1, NZ, sent_z, 0)
 
 
-STEP_AT = (0, 6, 14, 17, 23, 28, 36)
+STEP_AT = (0, 6, 14, 18, 23, 29, 36)
 
 
 def body(points, charges, leaf_density, leaf_octant, user_lists, near_leaves, near_codes,
@@ -513,22 +553,22 @@
             pltpu.VMEM((4, S, S), BF16),
             pltpu.VMEM((4, S, S), BF16),
             pltpu.VMEM((FAR, 48), BF16),
-            pltpu.VMEM((LB + 2, 8, PTS), F32),
+            pltpu.VMEM((LB + 2 * UH, 8, PTS), F32),
             pltpu.VMEM((LB + 2 * UH, PTS, 48), BF16),
             pltpu.VMEM((LB + 2 * UH, 16, PTS), BF16),
             pltpu.VMEM((2, 3, LB, PTS), F32),
             pltpu.VMEM((2, LB, Q, PTS), F32),
             pltpu.VMEM((LB, 16, PTS), F32),
-            pltpu.VMEM((2 * NG, ROWS + 8, SP), F32),
+            pltpu.VMEM((2 * NG, PACKED + 8, 128), F32),
             pltpu.VMEM((NG * NZ * Q, SP), F32),
             pltpu.VMEM((NG, NZ * Q, SP), F32),
             pltpu.VMEM((NZ, Q, SP), F32),
             pltpu.VMEM((NZ, Q, SP), F32),
             pltpu.VMEM((NZ, Q, SP), F32),
-            pltpu.VMEM((NZ * Q, SP), F32),
+            pltpu.VMEM((max(NZ * Q, ROWS), SP), F32),
             pltpu.VMEM((NG, NZ * Q + 8, SP), F32),
-            pltpu.VMEM((2 * NG, ROWS, SP), F32),
-            pltpu.VMEM((2 * NG, ROWS, SP), F32),
+            pltpu.VMEM((2 * NG, PACKED, 128), F32),
+            pltpu.VMEM((2 * NG, PACKED, 128), F32),
             pltpu.VMEM((LB // 2, 16, SP), BF16),
             pltpu.VMEM((LB, FAR, PTS), BF16),
             pltpu.VMEM((LB, FAR, PTS), BF16),

time: 70.3 us -> 67.8 us (0.964)
  Pallas kernels: 68.6 us -> 66.1 us
    pallas_call x1, Pallas kernels: 68.6 us -> 66.1 us  [body(): pl.pallas_call(kernel, out_shape=jax.ShapeDtypeStruct((LB, Q, PTS), F32),...]
where the time goes in v4:
time: 67.8 us; the launch traced here: 67.7 us
  Pallas kernels  66.1 us (97%)
  local copies, waits for them, and re-layouts  1.57 us (2%)
    pallas_call x1, Pallas kernels, body(): pl.pallas_call(kernel, out_shape=jax.ShapeDtypeStruct((LB, Q, PTS), F32),...  66.1 us
    unnamed x1, local copies, waits for them, and re-layouts  1.57 us

profile of v4, /device:TPU:1, one launch (start us, length us, event | category | flops | bytes accessed | tf_op | source)
XLA Modules:
  0.0 67.7 jit_solution(9299100418043536414)
XLA Ops:
  0.0 66.1 %shard_map.118 = f32[16,4,512]{2,1,0:T(4,128)} custom-call(s32[16]{0:T(128)} %octs.1, s32[2,4]{1,0:T(2,128)} %bitcast.7, s32[4,16]{1,0:T(4,128)} %bitcast.5, s32[4,16]{1,0:T(4,128)} %bitcast.6, f32[3,16,512]{2,1,0:T(8,128)} %bitcast.4, f32[16,4,512]{2,1,0:T(4,128)} %ch_in.1, f32[16,4,296]{2,1,0:T(4,128)} %dens_in.1, f32[296,296]{1,0:T(8,128)} %up_in.1, ...), custom_call_target="tpu_custom_call" | custom-call | tf_op jit(solution)/shard_map/pallas_call | solution.py:542
  66.1 1.6 %copy.14 = f32[16,4,512]{2,1,0:T(4,128)} copy(f32[16,4,512]{2,1,0:T(4,128)} %shard_map.118) | data formatting | bytes 262144

commit v5 on v4

--- a/solution.py
+++ b/solution.py
@@ -250,7 +250,7 @@
         prep(n, xp[n], ch[n] * INV_FOUR_PI)
         return 0
 
-    lax.fori_loop(0, LB // 2, prep_own, 0, unroll=2)
+    lax.fori_loop(0, LB // 2, prep_own, 0, unroll=4)
 
     n_wait = n_greet + (me + count - 1) // count + (2 * count - 2 - me) // count
     pl.semaphore_wait(barrier, n_wait)
@@ -413,21 +413,21 @@
             def _():
                 step()
 
-    lax.fori_loop(LB // 2, LB, prep_own, 0, unroll=2)
+    lax.fori_loop(LB // 2, LB, prep_own, 0, unroll=4)
     for i in range(3, 8):
         load(i).wait()
     fsurf[...] = surf[...].astype(BF16)
     for i in range(4):
         maps_hi[i], maps_lo[i] = split2(maps[i])
 
-    def own_pair(t, _):
-        for h in range(2):
-            l = 2 * t + h
+    def own_four(t, _):
+        for h in range(4):
+            l = 4 * t + h
             near[l] = pair_sum(fs[l], target_features(xp[l], row8), cw[l])
-        run_steps(2 * t)
+        run_steps(4 * t)
         return 0
 
-    lax.fori_loop(0, LB // 2, own_pair, 0)
+    lax.fori_loop(0, LB // 4, own_four, 0)
 
     for i in range(2):
         present = me > 0 if i == 0 else me < count - 1
@@ -452,7 +452,7 @@
             prep(at, xp[at], hc[i, n] * INV_FOUR_PI)
             return 0
 
-        lax.fori_loop(0, UH, prep_halo, 0, unroll=2)
+        lax.fori_loop(0, UH, prep_halo, 0, unroll=True)
 
     def near_leaf(l, _):
         acc = near[l]
@@ -531,7 +531,7 @@
     lax.fori_loop(1, NZ, sent_z, 0)
 
 
-STEP_AT = (0, 6, 14, 18, 23, 29, 36)
+STEP_AT = (0, 8, 12, 18, 23, 29, 36)
 
 
 def body(points, charges, leaf_density, leaf_octant, user_lists, near_leaves, near_codes,

time: 67.8 us -> 65.8 us (0.971)
  Pallas kernels: 66.1 us -> 64.1 us
    pallas_call x1, Pallas kernels: 66.1 us -> 64.1 us  [body(): pl.pallas_call(kernel, out_shape=jax.ShapeDtypeStruct((LB, Q, PTS), F32),...]
where the time goes in v5:
time: 65.8 us; the launch traced here: 65.7 us
  Pallas kernels  64.1 us (97%)
  local copies, waits for them, and re-layouts  1.57 us (2%)
    pallas_call x1, Pallas kernels, body(): pl.pallas_call(kernel, out_shape=jax.ShapeDtypeStruct((LB, Q, PTS), F32),...  64.1 us
    unnamed x1, local copies, waits for them, and re-layouts  1.57 us

profile of v5, /device:TPU:1, one launch (start us, length us, event | category | flops | bytes accessed | tf_op | source)
XLA Modules:
  0.0 65.7 jit_solution(1984491534817636180)
XLA Ops:
  0.0 64.1 %shard_map.118 = f32[16,4,512]{2,1,0:T(4,128)} custom-call(s32[16]{0:T(128)} %octs.1, s32[2,4]{1,0:T(2,128)} %bitcast.7, s32[4,16]{1,0:T(4,128)} %bitcast.5, s32[4,16]{1,0:T(4,128)} %bitcast.6, f32[3,16,512]{2,1,0:T(8,128)} %bitcast.4, f32[16,4,512]{2,1,0:T(4,128)} %ch_in.1, f32[16,4,296]{2,1,0:T(4,128)} %dens_in.1, f32[296,296]{1,0:T(8,128)} %up_in.1, ...), custom_call_target="tpu_custom_call" | custom-call | tf_op jit(solution)/shard_map/pallas_call | solution.py:542
  64.1 1.6 %copy.14 = f32[16,4,512]{2,1,0:T(4,128)} copy(f32[16,4,512]{2,1,0:T(4,128)} %shard_map.118) | data formatting | bytes 262144
